TPU v7x, 512 devices: a whole 4x4x16 slice. The times are simulated.
512 devices in a mesh: row: 16 (over x_lo, y, core), col: 32 (over x_hi, z).
Axes of the slice: x: 4 (x_hi: 2, x_lo: 2; x = x_hi * 2 + x_lo), y: 4, z: 16, core: 2. Of those that a mesh axis runs over, the one named last changes fastest.
Arguments:
- seq_ids: int32 [1024], replicated, may hold values from 0 to 3, never falling along the last dimension, each value on 1 to 512 neighbouring positions
- query_inputs: bfloat16 [1024, 8192], P('col', 'row'), may hold values from -6 to 6
- query_grads: bfloat16 [1024, 8192], P('row', 'col'), may hold values from -0.25 to 0.25
- query_act_basis: bfloat16 [8192, 8192], P('row', 'col'), may hold values from -0.0625 to 0.0625
- query_grad_basis: bfloat16 [8192, 8192], P('col', 'row'), may hold values from -0.0625 to 0.0625
- output_inputs: bfloat16 [1024, 8192], P('col', 'row'), may hold values from -6 to 6
- output_grads: bfloat16 [1024, 8192], P('row', 'col'), may hold values from -0.25 to 0.25
- output_act_basis: bfloat16 [8192, 8192], P('row', 'col'), may hold values from -0.0625 to 0.0625
- output_grad_basis: bfloat16 [8192, 8192], P('col', 'row'), may hold values from -0.0625 to 0.0625
Outputs:
- query_corr: float32 [8192, 8192], P('row', 'col')
- output_corr: float32 [8192, 8192], P('row', 'col')
Inputs may be any that keep to these rules, and one draw needn't show every extreme that they name: seq_ids never falls along the tokens; each of the 4 sequences holds 1 to 512 tokens, and one holds exactly 512.
All inputs are finite; a program needn't handle non-finite values.
Results may differ from a plain program's by a relative error of at most 0.0003.
Values may be sent and summed in bfloat16 or wider, within the bound.
No kernel may reach another device: no remote copies, remote signals or barrier semaphores. Data moves between devices by JAX's collectives and lax.ppermute only.
A program may use at most 64 MiB of HBM per device.

v0:
```python
import jax
import jax.numpy as jnp
from jax import lax
from jax.sharding import PartitionSpec as P

SEQS = 4
MOST = 512


def gather_act(inputs_now):
    return lax.all_gather(inputs_now, "col", axis=0, tiled=True)


def gather_grad(grads_now):
    return lax.all_gather(grads_now, "row", axis=0, tiled=True)


def reduce_act(partial_value):
    return lax.psum(partial_value, "row")


def reduce_grad(partial_value):
    return lax.psum(partial_value, "col")


def correct(act_rot, grad_rot, seq_ids):
    numbers = jnp.arange(SEQS, dtype=jnp.int32)
    counts = jnp.sum((seq_ids[None, :] == numbers[:, None]).astype(jnp.int32), axis=1)
    starts = jnp.cumsum(counts) - counts
    padded_act = jnp.concatenate([act_rot, jnp.zeros((MOST, act_rot.shape[1]), act_rot.dtype)], 0)
    padded_grad = jnp.concatenate(
        [grad_rot, jnp.zeros((MOST, grad_rot.shape[1]), grad_rot.dtype)], 0
    )
    offsets = jnp.arange(MOST, dtype=jnp.int32)
    running = jnp.zeros((grad_rot.shape[1], act_rot.shape[1]), jnp.float32)
    for seq_index in range(SEQS):
        act_rows = lax.dynamic_slice_in_dim(padded_act, starts[seq_index], MOST, 0)
        grad_rows = lax.dynamic_slice_in_dim(padded_grad, starts[seq_index], MOST, 0)
        inside = offsets < counts[seq_index]
        grad_rows = jnp.where(inside[:, None], grad_rows, jnp.zeros_like(grad_rows))
        product = lax.dot_general(
            grad_rows, act_rows, (((0,), (0,)), ((), ())), precision=lax.Precision.HIGHEST
        )
        running = running + product * product
    return running / SEQS


def act_term(gathered_act, act_eigen):
    return jnp.dot(gathered_act, act_eigen, preferred_element_type=jnp.float32)


def grad_term(gathered_grad, grad_eigen):
    return jnp.dot(gathered_grad, grad_eigen, preferred_element_type=jnp.float32)


def finish(seq_ids, gathered_act, gathered_grad, act_eigen, grad_eigen):
    act_rot = reduce_act(act_term(gathered_act, act_eigen))
    grad_rot = reduce_grad(grad_term(gathered_grad, grad_eigen))
    return correct(act_rot, grad_rot, seq_ids)


def per_device(
    seq_ids,
    query_inputs,
    query_grads,
    query_act_basis,
    query_grad_basis,
    output_inputs,
    output_grads,
    output_act_basis,
    output_grad_basis,
):
    projections = (
        (query_inputs, query_grads, query_act_basis, query_grad_basis),
        (output_inputs, output_grads, output_act_basis, output_grad_basis),
    )
    results = []
    for inputs_now, grads_now, act_eigen, grad_eigen in projections:
        results.append(
            finish(seq_ids, gather_act(inputs_now), gather_grad(grads_now), act_eigen, grad_eigen)
        )
    return (results[0], results[1])


def solution(mesh):
    in_specs = (
        P(),
        P("col", "row"),
        P("row", "col"),
        P("row", "col"),
        P("col", "row"),
        P("col", "row"),
        P("row", "col"),
        P("row", "col"),
        P("col", "row"),
    )
    out_specs = (P("row", "col"), P("row", "col"))
    return jax.shard_map(
        per_device, mesh=mesh, in_specs=in_specs, out_specs=out_specs, check_vma=False
    )
```

profile of v0, /device:TPU:8, one launch (start us, length us, event | category | flops | bytes accessed | tf_op | source)
XLA Modules:
  0.0 780.7 jit_solution(2244642291569405733)
XLA Ops:
  7.2 0.0 copy-start
  7.2 0.0 copy-start.5
  7.2 0.0 all-gather.3.cloned.1.call-start
  7.2 0.7 all-gather.3.cloned.1.call-update
  7.9 0.0 all-gather.5.cloned.1.call-start
  8.0 0.7 all-gather.5.cloned.1.call-update
  8.7 0.0 all-reduce.11.cloned.1.call-start
  8.7 149.8 %all-gather.3.cloned.1.call-done = bf16[1024,512]{1,0:T(8,128)(2,1)} async-done(((bf16[32,512]{1,0:T(8,128)(2,1)}), bf16[1024,512]{1,0:T(8,128)(2,1)}) %all-gather.3.cloned.1.call-update) | async-done | bytes 1048592 | tf_op jit(solution)/shard_map/all_gather | solution.py:11
  158.5 2.7 fusion.59
  161.2 0.0 copy-start.7
  161.2 0.0 copy-start.8
  161.2 137.7 %all-gather.5.cloned.1.call-done = bf16[1024,512]{1,0:T(8,128)(2,1)} async-done(((bf16[32,512]{1,0:T(8,128)(2,1)}), bf16[1024,512]{1,0:T(8,128)(2,1)}) %all-gather.5.cloned.1.call-update) | async-done | bytes 1048592 | tf_op jit(solution)/shard_map/all_gather | solution.py:11
  299.0 0.0 copy-done.5
  299.0 2.7 fusion.61
  301.6 0.0 all-reduce.11.cloned.1.call-update
  301.6 0.0 copy-start.6
  301.7 0.0 all-reduce.9.cloned.1.call-start
  301.7 0.0 copy-done.7
  301.7 17.9 %all_gather.12 = bf16[1024,256]{1,0:T(8,128)(2,1)S(1)} all-gather(bf16[64,256]{1,0:T(8,128)(2,1)S(1)} %copy-done.7), channel_id=1, replica_groups=mesh['row'=16,'col'=32] {'row'}, dimensions={0}, use_global_device_ids=true | all-gather | bytes 557056 | tf_op jit(solution)/shard_map/all_gather | solution.py:15
  319.6 0.0 copy-done.8
  319.6 20.3 %all_gather.14 = bf16[1024,256]{1,0:T(8,128)(2,1)S(1)} all-gather(bf16[64,256]{1,0:T(8,128)(2,1)S(1)} %copy-done.8), channel_id=1, replica_groups=mesh['row'=16,'col'=32] {'row'}, dimensions={0}, use_global_device_ids=true | all-gather | bytes 557056 | tf_op jit(solution)/shard_map/all_gather | solution.py:15
  340.0 0.0 copy-done
  340.0 1.8 fusion.58
  341.8 0.0 copy-done.6
  341.8 1.8 fusion.60
  343.5 0.0 copy-start.9
  343.5 0.0 all-reduce.9.cloned.1.call-update
  343.6 0.7 copy-done.9
  344.2 0.1 convert_reduce_fusion
  344.4 0.2 reduce-window.9
  344.5 0.7 fusion.57
  353.1 0.7 fusion.56
  353.7 0.6 iota_compare_fusion.3
  354.3 0.7 iota_compare_fusion.4
  355.0 0.7 iota_compare_fusion.2
  355.7 0.7 iota_compare_fusion.1
  356.4 76.7 %all-reduce.11.cloned.1.call-done = (f32[1024,256]{1,0:T(8,128)}, f32[1024,256]{1,0:T(8,128)}) async-done(((f32[1024,256]{1,0:T(8,128)}, f32[1024,256]{1,0:T(8,128)}), (f32[1024,256]{1,0:T(8,128)}, f32[1024,256]{1,0:T(8,128)})) %all-reduce.11.cloned.1.call-update) | async-done | bytes 2097168 | tf_op jit(solution)/shard_map/psum | solution.py:19
  433.1 0.0 copy-start.3
  433.1 322.2 %all-reduce.9.cloned.1.call-done = (f32[1024,512]{1,0:T(8,128)}, f32[1024,512]{1,0:T(8,128)}) async-done(((f32[1024,512]{1,0:T(8,128)}, f32[1024,512]{1,0:T(8,128)}), (f32[1024,512]{1,0:T(8,128)}, f32[1024,512]{1,0:T(8,128)})) %all-reduce.9.cloned.1.call-update) | async-done | bytes 4194320 | tf_op jit(solution)/shard_map/psum | solution.py:23
  755.2 0.0 copy-start.1
  755.2 3.4 convolution_multiply_fusion.6
  758.7 0.0 copy-start.2
  758.7 0.0 copy-start.4
  758.7 0.0 copy-done.3
  758.7 0.0 copy-done.1
  758.7 1.9 convolution_multiply_fusion.2
  760.7 0.0 copy-done.2
  760.7 0.0 copy-done.4
  760.7 1.9 fusion
  762.6 1.9 fusion.3
  764.6 1.9 fusion.1
  766.5 2.1 fusion.4
  768.7 2.7 fusion.7
  771.4 2.7 fusion.6
  (1 shorter events, 0.0 us)
Async XLA Ops:
  7.2 332.8 %copy-start = (bf16[256,512]{1,0:T(8,128)(2,1)S(1)}, bf16[256,512]{1,0:T(8,128)(2,1)}, u32[]{:S(2)}) copy-start(bf16[256,512]{1,0:T(8,128)(2,1)} %param.13) | copy-start | bytes 786436
  7.2 291.8 %copy-start.5 = (bf16[512,256]{1,0:T(8,128)(2,1)S(1)}, bf16[512,256]{1,0:T(8,128)(2,1)}, u32[]{:S(2)}) copy-start(bf16[512,256]{1,0:T(8,128)(2,1)} %param.16) | copy-start | bytes 786436
  7.2 151.3 %all-gather.3.cloned.1.call-start = ((), (), s32[]{:S(2)}) async-start(), calls=%async_computation | async-start | bytes 1081344 | tf_op jit(solution)/shard_map/all_gather | solution.py:11
  7.9 291.0 %all-gather.5.cloned.1.call-start = ((), (), s32[]{:S(2)}) async-start(), calls=%async_computation.1 | async-start | bytes 1081344 | tf_op jit(solution)/shard_map/all_gather | solution.py:11
  8.7 424.4 %all-reduce.11.cloned.1.call-start = ((), (), s32[]{:S(2)}) async-start(), calls=%async_computation.3 | async-start | bytes 4194304 | tf_op jit(solution)/shard_map/psum | solution.py:19
  161.2 140.5 %copy-start.7 = (bf16[64,256]{1,0:T(8,128)(2,1)S(1)}, bf16[64,256]{1,0:T(8,128)(2,1)}, u32[]{:S(2)}) copy-start(bf16[64,256]{1,0:T(8,128)(2,1)} %param.11) | copy-start | bytes 98308
  161.2 158.4 %copy-start.8 = (bf16[64,256]{1,0:T(8,128)(2,1)S(1)}, bf16[64,256]{1,0:T(8,128)(2,1)}, u32[]{:S(2)}) copy-start(bf16[64,256]{1,0:T(8,128)(2,1)} %param.15) | copy-start | bytes 98308
  301.6 40.1 %copy-start.6 = (bf16[256,512]{1,0:T(8,128)(2,1)S(1)}, bf16[256,512]{1,0:T(8,128)(2,1)}, u32[]{:S(2)}) copy-start(bf16[256,512]{1,0:T(8,128)(2,1)} %param.17) | copy-start | bytes 786436
  301.7 453.6 %all-reduce.9.cloned.1.call-start = ((), (), s32[]{:S(2)}) async-start(), calls=%async_computation.2 | async-start | bytes 8388608 | tf_op jit(solution)/shard_map/psum | solution.py:23
  343.5 0.7 copy-start.9
  433.1 325.6 %copy-start.3 = (f32[1024,256]{1,0:T(8,128)S(1)}, f32[1024,256]{1,0:T(8,128)}, u32[]{:S(2)}) copy-start(f32[1024,256]{1,0:T(8,128)} %get-tuple-element.5) | copy-start | bytes 3145732
  755.2 3.5 copy-start.1
  758.7 2.0 copy-start.2
  758.7 2.0 copy-start.4
Sparse Core Ops, SparseCore 0:
  11.1 147.3 all-gather.2
  161.6 137.2 all-gather.4
  301.9 131.0 all-reduce.10
  435.9 319.2 all-reduce.8
where the time goes:
time: 781 us
  waiting for transfers between devices  688 us (88%)
  blocking collectives  38.2 us (5%)
  matrix products  27.7 us (4%)
  between operations  21.8 us (3%)
    psum x1, waiting for transfers between devices, reduce_grad(): return lax.psum(partial_value, 'col')  322 us
    all_gather x2, waiting for transfers between devices, gather_act(): return lax.all_gather(inputs_now, 'col', axis=0, tiled=True)  288 us
    psum x1, waiting for transfers between devices, reduce_act(): return lax.psum(partial_value, 'row')  76.7 us
    all_gather x2, blocking collectives, gather_grad(): return lax.all_gather(grads_now, 'row', axis=0, tiled=True)  38.2 us
    dot_general x8, matrix products, correct(): lax.dot_general(grad_rows, act_rows, (((0,), (0,)), ((), ())), precision=...  18.8 us
  transfers between devices with their start and end apart: 4, of which 4 were waited for; matrix products, arithmetic and copies ran while one was open for 1% of the time, Pallas kernels for 0%

commit v1 on v0

--- a/solution.py
+++ b/solution.py
@@ -8,7 +8,9 @@
 
 
 def gather_act(inputs_now):
-    return lax.all_gather(inputs_now, "col", axis=0, tiled=True)
+    return jnp.concatenate(
+        lax.all_to_all(jnp.stack([inputs_now] * lax.axis_size("col")), "col", 0, 0), axis=0
+    )
 
 
 def gather_grad(grads_now):

time: 781 us -> 581 us (0.74)
  the two profiles are of different devices: /device:TPU:8 before, /device:TPU:1 now
where the time goes in v1:
time: 581 us
  waiting for transfers between devices  457 us (79%)
  blocking collectives  39.9 us (7%)
  starting transfers between devices  27.9 us (5%)
  matrix products  25.2 us (4%)
  between operations  22.1 us (4%)
    psum x1, waiting for transfers between devices, reduce_grad(): return lax.psum(partial_value, 'col')  240 us
    psum x1, waiting for transfers between devices, reduce_act(): return lax.psum(partial_value, 'row')  154 us
    all_to_all x2, waiting for transfers between devices, gather_act(): lax.all_to_all(jnp.stack([inputs_now] * lax.axis_size('col')), 'col', 0, 0)  62.9 us
    all_gather x2, blocking collectives, gather_grad(): return lax.all_gather(grads_now, 'row', axis=0, tiled=True)  39.9 us
    all_to_all x2, starting transfers between devices, gather_act(): lax.all_to_all(jnp.stack([inputs_now] * lax.axis_size('col')), 'col', 0, 0)  27.6 us
    dot_general x8, matrix products, correct(): lax.dot_general(grad_rows, act_rows, (((0,), (0,)), ((), ())), precision=...  18.8 us
  transfers between devices with their start and end apart: 4, of which 4 were waited for; matrix products, arithmetic and copies ran while one was open for 2% of the time, Pallas kernels for 0%

profile of v1, /device:TPU:1, one launch (start us, length us, event | category | flops | bytes accessed | tf_op | source)
XLA Modules:
  0.0 580.6 jit_solution(18147329845206834547)
XLA Ops:
  7.2 0.0 copy-start
  7.2 0.0 copy-start.8
  7.2 0.0 copy-start.9
  7.2 1.9 stack.4
  9.1 18.5 %all-to-all-start = ((bf16[32,32,512]{2,1,0:T(8,128)(2,1)}), bf16[32,32,512]{2,1,0:T(8,128)(2,1)S(1)}, u32[]{:S(2)}, u32[]{:S(2)}) async-start(bf16[32,32,512]{2,1,0:T(8,128)(2,1)} %stack.4), calls=%async_computation | async-start | bytes 2097152 | tf_op jit(solution)/shard_map/all_to_all | solution.py:12
  27.6 0.0 copy-done.8
  27.6 0.0 copy-start.10
  27.6 21.7 %all_gather.6 = bf16[1024,256]{1,0:T(8,128)(2,1)S(1)} all-gather(bf16[64,256]{1,0:T(8,128)(2,1)S(1)} %copy-done.8), channel_id=1, replica_groups=mesh['row'=16,'col'=32] {'row'}, dimensions={0}, use_global_device_ids=true | all-gather | bytes 557056 | tf_op jit(solution)/shard_map/all_gather | solution.py:17
  49.3 0.0 copy-done.9
  49.3 18.3 %all_gather.7 = bf16[1024,256]{1,0:T(8,128)(2,1)S(1)} all-gather(bf16[64,256]{1,0:T(8,128)(2,1)S(1)} %copy-done.9), channel_id=1, replica_groups=mesh['row'=16,'col'=32] {'row'}, dimensions={0}, use_global_device_ids=true | all-gather | bytes 557056 | tf_op jit(solution)/shard_map/all_gather | solution.py:17
  67.6 0.0 copy-done
  67.6 1.8 fusion.58
  69.3 0.0 copy-start.7
  69.3 9.5 %all-to-all-done = bf16[32,32,512]{2,1,0:T(8,128)(2,1)S(1)} async-done(((bf16[32,32,512]{2,1,0:T(8,128)(2,1)}), bf16[32,32,512]{2,1,0:T(8,128)(2,1)S(1)}, u32[]{:S(2)}, u32[]{:S(2)}) %all-to-all-start) | async-done | bytes 1048608 | tf_op jit(solution)/shard_map/all_to_all | solution.py:12
  78.8 0.0 copy-done.10
  78.8 1.2 stack.5
  80.0 9.2 %all-to-all-start.1 = ((bf16[32,32,512]{2,1,0:T(8,128)(2,1)}), bf16[32,32,512]{2,1,0:T(8,128)(2,1)S(1)}, u32[]{:S(2)}, u32[]{:S(2)}) async-start(bf16[32,32,512]{2,1,0:T(8,128)(2,1)} %stack.5), calls=%async_computation.1 | async-start | bytes 2097152 | tf_op jit(solution)/shard_map/all_to_all | solution.py:12
  89.2 0.0 all-reduce.9.cloned.1.call-start
  89.2 0.0 copy-done.7
  89.2 1.8 fusion.60
  91.0 0.0 copy-start.5
  91.0 0.0 all-reduce.9.cloned.1.call-update
  91.0 0.0 copy-start.6
  91.0 0.2 all-reduce.11.cloned.1.call-start
  91.3 0.7 copy-done.5
  92.0 1.4 fusion.59
  93.4 53.4 %all-to-all-done.1 = bf16[32,32,512]{2,1,0:T(8,128)(2,1)S(1)} async-done(((bf16[32,32,512]{2,1,0:T(8,128)(2,1)}), bf16[32,32,512]{2,1,0:T(8,128)(2,1)S(1)}, u32[]{:S(2)}, u32[]{:S(2)}) %all-to-all-start.1) | async-done | bytes 1048608 | tf_op jit(solution)/shard_map/all_to_all | solution.py:12
  146.8 0.0 copy-done.6
  146.8 0.0 copy-start.11
  146.8 1.4 fusion.61
  148.3 0.0 all-reduce.11.cloned.1.call-update
  148.3 0.0 copy-done.11
  148.3 0.1 convert_reduce_fusion
  148.4 0.2 reduce-window.9
  148.6 0.7 fusion.57
  157.1 0.7 fusion.56
  157.8 0.6 iota_compare_fusion.3
  158.4 0.7 iota_compare_fusion.4
  159.1 0.7 iota_compare_fusion.2
  159.8 0.7 iota_compare_fusion.1
  160.4 240.2 %all-reduce.9.cloned.1.call-done = (f32[1024,512]{1,0:T(8,128)}, f32[1024,512]{1,0:T(8,128)}) async-done(((f32[1024,512]{1,0:T(8,128)}, f32[1024,512]{1,0:T(8,128)}), (f32[1024,512]{1,0:T(8,128)}, f32[1024,512]{1,0:T(8,128)})) %all-reduce.9.cloned.1.call-update) | async-done | bytes 4194320 | tf_op jit(solution)/shard_map/psum | solution.py:25
  400.6 0.0 copy-start.1
  400.6 154.3 %all-reduce.11.cloned.1.call-done = (f32[1024,256]{1,0:T(8,128)}, f32[1024,256]{1,0:T(8,128)}) async-done(((f32[1024,256]{1,0:T(8,128)}, f32[1024,256]{1,0:T(8,128)}), (f32[1024,256]{1,0:T(8,128)}, f32[1024,256]{1,0:T(8,128)})) %all-reduce.11.cloned.1.call-update) | async-done | bytes 2097168 | tf_op jit(solution)/shard_map/psum | solution.py:21
  554.9 0.0 copy-start.3
  554.9 3.4 convolution_multiply_fusion.6
  558.3 0.0 copy-start.2
  558.3 0.0 copy-start.4
  558.3 0.0 copy-done.1
  558.3 0.0 copy-done.3
  558.3 1.9 convolution_multiply_fusion.2
  560.3 0.0 copy-done.2
  560.3 0.0 copy-done.4
  560.3 1.9 fusion
  562.2 1.9 fusion.3
  564.2 1.9 fusion.1
  566.1 2.2 fusion.4
  568.3 2.7 fusion.7
  571.1 2.7 fusion.6
  (1 shorter events, 0.0 us)
Async XLA Ops:
  7.2 60.4 %copy-start = (bf16[256,512]{1,0:T(8,128)(2,1)S(1)}, bf16[256,512]{1,0:T(8,128)(2,1)}, u32[]{:S(2)}) copy-start(bf16[256,512]{1,0:T(8,128)(2,1)} %param.13) | copy-start | bytes 786436
  7.2 20.4 %copy-start.8 = (bf16[64,256]{1,0:T(8,128)(2,1)S(1)}, bf16[64,256]{1,0:T(8,128)(2,1)}, u32[]{:S(2)}) copy-start(bf16[64,256]{1,0:T(8,128)(2,1)} %param.11) | copy-start | bytes 98308
  7.2 42.1 %copy-start.9 = (bf16[64,256]{1,0:T(8,128)(2,1)S(1)}, bf16[64,256]{1,0:T(8,128)(2,1)}, u32[]{:S(2)}) copy-start(bf16[64,256]{1,0:T(8,128)(2,1)} %param.15) | copy-start | bytes 98308
  9.1 69.7 %all-to-all-start = ((bf16[32,32,512]{2,1,0:T(8,128)(2,1)}), bf16[32,32,512]{2,1,0:T(8,128)(2,1)S(1)}, u32[]{:S(2)}, u32[]{:S(2)}) async-start(bf16[32,32,512]{2,1,0:T(8,128)(2,1)} %stack.4), calls=%async_computation | async-start | bytes 2097152 | tf_op jit(solution)/shard_map/all_to_all | solution.py:12
  27.6 51.2 %copy-start.10 = (bf16[32,512]{1,0:T(8,128)(2,1)S(1)}, bf16[32,512]{1,0:T(8,128)(2,1)}, u32[]{:S(2)}) copy-start(bf16[32,512]{1,0:T(8,128)(2,1)} %param.14) | copy-start | bytes 98308
  69.3 19.9 %copy-start.7 = (bf16[256,512]{1,0:T(8,128)(2,1)S(1)}, bf16[256,512]{1,0:T(8,128)(2,1)}, u32[]{:S(2)}) copy-start(bf16[256,512]{1,0:T(8,128)(2,1)} %param.17) | copy-start | bytes 786436
  80.0 66.8 %all-to-all-start.1 = ((bf16[32,32,512]{2,1,0:T(8,128)(2,1)}), bf16[32,32,512]{2,1,0:T(8,128)(2,1)S(1)}, u32[]{:S(2)}, u32[]{:S(2)}) async-start(bf16[32,32,512]{2,1,0:T(8,128)(2,1)} %stack.5), calls=%async_computation.1 | async-start | bytes 2097152 | tf_op jit(solution)/shard_map/all_to_all | solution.py:12
  89.2 311.5 %all-reduce.9.cloned.1.call-start = ((), (), s32[]{:S(2)}) async-start(), calls=%async_computation.2 | async-start | bytes 8388608 | tf_op jit(solution)/shard_map/psum | solution.py:25
  91.0 0.9 copy-start.5
  91.0 55.8 %copy-start.6 = (bf16[512,256]{1,0:T(8,128)(2,1)S(1)}, bf16[512,256]{1,0:T(8,128)(2,1)}, u32[]{:S(2)}) copy-start(bf16[512,256]{1,0:T(8,128)(2,1)} %param.16) | copy-start | bytes 786436
  91.0 463.8 %all-reduce.11.cloned.1.call-start = ((), (), s32[]{:S(2)}) async-start(), calls=%async_computation.3 | async-start | bytes 4194304 | tf_op jit(solution)/shard_map/psum | solution.py:21
  146.8 1.5 copy-start.11
  400.6 157.7 %copy-start.1 = (f32[1024,512]{1,0:T(8,128)S(1)}, f32[1024,512]{1,0:T(8,128)}, u32[]{:S(2)}) copy-start(f32[1024,512]{1,0:T(8,128)} %get-tuple-element.3) | copy-start | bytes 6291460
  554.9 3.4 copy-start.3
  558.3 2.0 copy-start.2
  558.3 2.0 copy-start.4
Sparse Core Ops, SparseCore 0:
  93.0 307.6 all-reduce.8
  403.6 151.2 all-reduce.10
